TPU v7x, 32 devices: a whole 2x2x4 slice. The times are simulated.
32 devices in a mesh: ctx: 4 (over y, x), frame: 8 (over z, core).
Axes of the slice: x: 2, y: 2, z: 4, core: 2. Of those that a mesh axis runs over, the one named last changes fastest.
Arguments:
- queries: bfloat16 [1024, 2048], P('ctx', 'frame'), may hold values from -160 to 160
- keys: bfloat16 [4096, 2048], P('ctx', 'frame'), may hold values from -4 to 4
- values: bfloat16 [4096, 2048], P('ctx', 'frame'), may hold values from -6 to 6
- query_frames: int32 [64], P('ctx'), may hold values from 0 to 191, as said below
- frame_counts: int32 [256], replicated, may hold values from 0 to 16, as said below
- clip_of_frame: int32 [64], P('ctx'), may hold values from 0 to 7, as said below
- in_proj: bfloat16 [2048, 1024], P('frame'), may hold values from -0.125 to 0.125
- mlp_up: bfloat16 [1024, 4096], replicated, may hold values from -0.1875 to 0.1875
- mlp_down: bfloat16 [4096, 1024], replicated, may hold values from -0.09375 to 0.09375
- reward_head: float32 [1024], replicated, may hold values from -0.1875 to 0.1875
Outputs:
- query_grad: float32 [1024, 2048], P('ctx', 'frame')
- key_grad: float32 [4096, 2048], P('ctx', 'frame')
- value_grad: float32 [4096, 2048], P('ctx', 'frame')
- clip_reward: float32 [32], P(('ctx', 'frame'))
Inputs may be any that keep to these rules, and one draw needn't show every extreme that they name: `query_frames`: the query patch rows are distinct rows of the first 256 * 3 // 4 patch rows of the video, in increasing order, all of them live; the first and the last of those rows are always among them. `frame_counts`: the live tokens are a prefix of the sequence of at least three quarters of it: rows before the prefix's end are full, one row may be partly live, the rows after it have none, and the last row has none. `clip_of_frame`: within each aligned block of 16 patch row slots every clip number appears exactly 2 times.
All inputs are finite; a program needn't handle non-finite values.
Results may differ from a plain program's by a relative error of at most 0.02.
Values may be sent and summed in bfloat16 or wider, within the bound.
A program may use at most 192 MiB of HBM per device.

v0:
```python
import functools
import math

import jax
import jax.numpy as jnp
from jax import lax
from jax.sharding import PartitionSpec as P

HD = 128
FTOK = 16
CLIP = 2


EPSILON = 1e-05


def rotate(values_in, position, inverse):
    row_count = values_in.shape[0]
    half_width = HD // 2
    pieces = values_in.reshape(row_count, -1, HD)
    frequency = jnp.exp(-math.log(10000.0) * jnp.arange(half_width, dtype=jnp.float32) / half_width)
    angle = position.astype(jnp.float32)[:, None] * frequency[None, :]
    cosine = jnp.cos(angle)[:, None, :]
    sine = jnp.sin(angle)[:, None, :]
    if inverse:
        sine = -sine
    first_half = pieces[:, :, :half_width]
    second_half = pieces[:, :, half_width:]
    result = jnp.concatenate(
        [first_half * cosine - second_half * sine, second_half * cosine + first_half * sine], axis=2
    )
    return result.reshape(row_count, -1)


def normalize(values_in):
    center = jnp.mean(values_in, axis=-1, keepdims=True)
    centered = values_in - center
    variance = jnp.mean(centered * centered, axis=-1, keepdims=True)
    return centered * lax.rsqrt(variance + EPSILON)


def head_scores(query_head, key_head, key_valid):
    scores = jnp.dot(query_head, key_head.T, preferred_element_type=jnp.float32) * (
        1.0 / math.sqrt(HD)
    )
    return jnp.where(key_valid[None, :], scores, -jnp.inf)


def contract_rows(left, right):
    return lax.dot_general(
        left, right, (((0,), (0,)), ((), ())), preferred_element_type=jnp.float32
    )


def score_clip(inputs, clip_live, mlp_up, mlp_down, reward_head):
    normed = normalize(inputs).astype(jnp.bfloat16)
    expanded = jax.nn.gelu(jnp.dot(normed, mlp_up, preferred_element_type=jnp.float32)).astype(
        jnp.bfloat16
    )
    hidden = jnp.dot(expanded, mlp_down, preferred_element_type=jnp.float32)
    live = clip_live.astype(jnp.float32)
    count = jnp.sum(live)
    pooled = jnp.sum(hidden * live[:, None], axis=0) / count
    return count * jnp.dot(normalize(pooled), reward_head, precision=lax.Precision.HIGHEST)


def shards(
    queries,
    keys,
    values,
    query_frames,
    frame_counts,
    clip_of_frame,
    in_proj,
    mlp_up,
    mlp_down,
    reward_head,
):
    ctx_index = lax.axis_index("ctx")
    frame_index = lax.axis_index("frame")
    query_rows = queries.shape[0]
    key_rows = keys.shape[0]
    frame_slots = query_frames.shape[0]
    width_dev = queries.shape[1]
    head_count = width_dev // HD
    key_frames = frame_counts.shape[0]
    scale = 1.0 / math.sqrt(HD)
    in_frame = jnp.arange(FTOK, dtype=jnp.int32)
    query_position = (query_frames[:, None] * FTOK + in_frame[None, :]).reshape(-1)
    key_position = ctx_index * key_rows + jnp.arange(key_rows, dtype=jnp.int32)
    key_valid = (in_frame[None, :] < frame_counts[:, None]).reshape(-1)
    frame_match = query_frames[:, None] == jnp.arange(key_frames, dtype=jnp.int32)[None, :]
    slot_counts = jnp.sum(jnp.where(frame_match, frame_counts[None, :], 0), axis=1)
    rotated_query = rotate(queries.astype(jnp.float32), query_position, False).astype(jnp.bfloat16)
    rotated_key = rotate(keys.astype(jnp.float32), key_position, False).astype(jnp.bfloat16)
    whole_key, whole_value = (
        lax.all_gather(rotated_key, "ctx", axis=0, tiled=True),
        lax.all_gather(values, "ctx", axis=0, tiled=True),
    )
    out_list, log_list, weight_list = ([], [], [])
    for head_number in range(head_count):
        lower = head_number * HD
        scores = head_scores(
            rotated_query[:, lower : lower + HD], whole_key[:, lower : lower + HD], key_valid
        )
        largest = jnp.max(scores, axis=1)
        total = jnp.sum(jnp.exp(scores - largest[:, None]), axis=1)
        log_total = largest + jnp.log(total)
        weights = jnp.exp(scores - log_total[:, None])
        out_list.append(
            jnp.dot(
                weights.astype(jnp.bfloat16),
                whole_value[:, lower : lower + HD],
                preferred_element_type=jnp.float32,
            ).astype(jnp.bfloat16)
        )
        log_list.append(log_total)
        weight_list.append(weights)
    attention_out = jnp.concatenate(out_list, axis=1)
    slot_index = jnp.arange(frame_slots, dtype=jnp.int32)
    same_clip = clip_of_frame[:, None] == clip_of_frame[None, :]
    earlier = slot_index[None, :] < slot_index[:, None]
    rank = jnp.sum(jnp.logical_and(same_clip, earlier), axis=1)
    destination = clip_of_frame * CLIP + rank
    source = jnp.sum(
        jnp.where(destination[None, :] == slot_index[:, None], slot_index[None, :], 0), axis=1
    )

    def regroup(array, order):
        framed = array.reshape(frame_slots, FTOK, array.shape[1])
        return jnp.take(framed, order, axis=0).reshape(query_rows, array.shape[1])

    grouped_out = regroup(attention_out, source)
    my_slots = lax.dynamic_slice_in_dim(source, frame_index * CLIP, CLIP)
    my_match = my_slots[:, None] == slot_index[None, :]
    my_counts = jnp.sum(jnp.where(my_match, slot_counts[None, :], 0), axis=1)
    clip_live = (in_frame[None, :] < my_counts[:, None]).reshape(-1)
    clip_inputs = lax.psum_scatter(
        jnp.dot(grouped_out, in_proj, preferred_element_type=jnp.float32),
        "frame",
        scatter_dimension=0,
        tiled=True,
    )
    scorer = functools.partial(
        score_clip, clip_live=clip_live, mlp_up=mlp_up, mlp_down=mlp_down, reward_head=reward_head
    )
    clip_value, pull_back = jax.vjp(scorer, clip_inputs)
    (input_grad,) = pull_back(jnp.ones_like(clip_value))
    low_grad = input_grad.astype(jnp.bfloat16)
    grouped_grad = jnp.dot(
        lax.all_gather(low_grad, "frame", axis=0, tiled=True),
        in_proj.T,
        preferred_element_type=jnp.float32,
    ).astype(jnp.bfloat16)
    out_grad = regroup(grouped_grad, destination)
    delta_list = []
    for head_number in range(head_count):
        lower = head_number * HD
        delta_list.append(
            jnp.sum(
                out_grad[:, lower : lower + HD].astype(jnp.float32)
                * attention_out[:, lower : lower + HD].astype(jnp.float32),
                axis=1,
            )
        )
    log_stack = jnp.stack(log_list, axis=1)
    delta_stack = jnp.stack(delta_list, axis=1)
    whole_query, whole_out_grad = (
        lax.all_gather(rotated_query, "ctx", axis=0, tiled=True),
        lax.all_gather(out_grad, "ctx", axis=0, tiled=True),
    )
    whole_log, whole_delta = (
        lax.all_gather(log_stack, "ctx", axis=0, tiled=True),
        lax.all_gather(delta_stack, "ctx", axis=0, tiled=True),
    )
    own_valid = lax.dynamic_slice_in_dim(key_valid, ctx_index * key_rows, key_rows)
    key_parts, value_parts, grad_list = ([], [], [])
    for head_number in range(head_count):
        lower = head_number * HD
        query_head = whole_query[:, lower : lower + HD]
        grad_head = whole_out_grad[:, lower : lower + HD]
        scores = head_scores(query_head, rotated_key[:, lower : lower + HD], own_valid)
        weights = jnp.exp(scores - whole_log[:, head_number][:, None])
        weight_grad = jnp.dot(
            grad_head, values[:, lower : lower + HD].T, preferred_element_type=jnp.float32
        )
        score_grad = (
            weights * (weight_grad - whole_delta[:, head_number][:, None]) * scale
        ).astype(jnp.bfloat16)
        key_parts.append(contract_rows(score_grad, query_head))
        value_parts.append(contract_rows(weights.astype(jnp.bfloat16), grad_head))
        grad_list.append(score_grad)
    rotated_key_grad = jnp.concatenate(key_parts, axis=1)
    value_grad = jnp.concatenate(value_parts, axis=1)
    query_parts = []
    for head_number in range(head_count):
        lower = head_number * HD
        grad_rows = grad_list[head_number]
        query_parts.append(
            jnp.dot(
                grad_rows, rotated_key[:, lower : lower + HD], preferred_element_type=jnp.float32
            )
        )
    rotated_query_grad = lax.psum_scatter(
        jnp.concatenate(query_parts, axis=1), "ctx", scatter_dimension=0, tiled=True
    )
    query_grad = rotate(rotated_query_grad, query_position, True)
    key_grad = rotate(rotated_key_grad, key_position, True)
    return (query_grad, key_grad, value_grad, clip_value.reshape(1))


def solution(mesh):
    return jax.shard_map(
        shards,
        mesh=mesh,
        in_specs=(
            P("ctx", "frame"),
            P("ctx", "frame"),
            P("ctx", "frame"),
            P("ctx"),
            P(),
            P("ctx"),
            P("frame", None),
            P(),
            P(),
            P(),
        ),
        out_specs=(P("ctx", "frame"), P("ctx", "frame"), P("ctx", "frame"), P(("ctx", "frame"))),
        check_vma=False,
    )
```

profile of v0, /device:TPU:0, one launch (start us, length us, event | category | flops | bytes accessed | tf_op | source)
XLA Modules:
  0.0 239.7 jit_solution(12190452999507283694)
XLA Ops:
  13.5 36.2 %all-gather.3.cloned.1.call-done = bf16[4096,256]{0,1:T(8,128)(2,1)} async-done(((bf16[1024,256]{0,1:T(8,128)(2,1)}), bf16[4096,256]{0,1:T(8,128)(2,1)}) %all-gather.3.cloned.1.call-update) | async-done | bytes 2097168 | tf_op jit(solution)/shard_map/all_gather | solution.py:97
  49.6 2.2 fusion.110
  53.8 2.0 copy-done.2
  56.5 30.3 %all-gather.5.cloned.1.call-done = bf16[4096,256]{1,0:T(8,128)(2,1)} async-done(((bf16[1024,256]{1,0:T(8,128)(2,1)}), bf16[4096,256]{1,0:T(8,128)(2,1)}) %all-gather.5.cloned.1.call-update) | async-done | bytes 2097168 | tf_op jit(solution)/shard_map/all_gather | solution.py:98
  86.8 3.6 %fusion.16 = bf16[256,128]{0,1:T(8,128)(2,1)S(1)} fusion(f32[256,4096]{1,0:T(8,128)} %copy-done.1, f32[256]{0:T(256)S(1)} %log_add_fusion.1, bf16[4096,256]{1,0:T(8,128)(2,1)} %all-gather.5.cloned.1.call-done), kind=kOutput, calls=%fused_computation.29 | convolution fusion | flops 270565376 | bytes 5309440 | tf_op jit(solution)/shard_map/dot_general | solution.py:111
  90.6 2.3 fusion.15
  95.6 13.4 %all_gather.21 = bf16[1024,256]{0,1:T(8,128)(2,1)S(1)} all-gather(bf16[256,256]{0,1:T(8,128)(2,1)S(1)} %bitcast.47), channel_id=1, replica_groups=mesh['ctx'=4,'frame'=8] {'ctx'}, dimensions={0}, use_global_device_ids=true | all-gather | bytes 655360 | tf_op jit(solution)/shard_map/all_gather | solution.py:169
  109.7 2.7 %fusion.67 = f32[1024,1024]{1,0:T(8,128)} fusion(bf16[1024,256]{0,1:T(8,128)(2,1)S(1)} %bitcast.38, bf16[1024,256]{0,1:T(8,128)(2,1)S(1)} %all_gather.21), kind=kOutput, calls=%fused_computation.94 | convolution fusion | flops 268435456 | bytes 4718592 | tf_op jit(solution)/shard_map/dot_general | solution.py:43
  112.4 2.7 %fusion.58 = f32[1024,1024]{1,0:T(8,128)} fusion(bf16[1024,256]{0,1:T(8,128)(2,1)S(1)} %bitcast.39, bf16[1024,256]{0,1:T(8,128)(2,1)S(1)} %all_gather.21), kind=kOutput, calls=%fused_computation.85 | convolution fusion | flops 268435456 | bytes 4718592 | tf_op jit(solution)/shard_map/dot_general | solution.py:43
  115.1 7.3 %all_gather.23 = f32[1024,2]{0,1:T(2,128)S(1)} all-gather(f32[256,2]{0,1:T(2,128)S(1)} %pad_maximum_fusion.8), channel_id=1, replica_groups=mesh['ctx'=4,'frame'=8] {'ctx'}, dimensions={0}, use_global_device_ids=true | all-gather | bytes 10240 | tf_op jit(solution)/shard_map/all_gather | solution.py:173
  122.4 5.0 %reduce-scatter.3.cloned.1.call-done = f32[32,1024]{1,0:T(8,128)} async-done(((f32[256,1024]{1,0:T(8,128)}), f32[32,1024]{1,0:T(8,128)}) %reduce-scatter.3.cloned.1.call-update) | async-done | bytes 131088 | tf_op jit(solution)/shard_map/reduce_scatter | solution.py:138
  129.6 5.0 %fusion.75 = f32[32,4096]{1,0:T(8,128)S(1)} fusion(bf16[1024,4096]{1,0:T(8,128)(2,1)} %param.19, f32[32,1024]{1,0:T(8,128)} %reduce-scatter.3.cloned.1.call-done, f32[32]{0:T(128)S(1)} %fusion.87, f32[32]{0:T(128)S(1)} %broadcast_multiply_fusion), kind=kOutput, calls=%fused_computation.119 | convolution fusion | flops 268533760 | bytes 9044224 | tf_op jit(solution)/shard_map/jvp()/dot_general | solution.py:57
  134.6 4.9 %fusion.18 = f32[1024]{0:T(1024)S(1)} fusion(bf16[4096,1024]{1,0:T(8,128)(2,1)} %param.20, f32[32,4096]{1,0:T(8,128)S(1)} %fusion.75, f32[32]{0:T(128)S(1)} %reshape.360), kind=kOutput, calls=%fused_computation.32 | convolution fusion | flops 269679616 | bytes 8917120 | tf_op jit(solution)/shard_map/jvp()/dot_general | solution.py:60
  148.2 11.0 %multiply_reduce_fusion.2 = (f32[32]{0:T(128)S(1)}, f32[32,1024]{1,0:T(8,128)S(1)}) fusion(f32[32,1024]{1,0:T(8,128)S(1)} %copy-done.8, f32[32]{0:T(128)S(1)} %broadcast_multiply_fusion, bf16[1024,4096]{1,0:T(8,128)(2,1)} %param.19, f32[32,4096]{1,0:T(8,128)S(1)} %fusion.75, bf16[4096,1024]{1,0:T(8,128)(2,1)} %param.20, f32[1024]{0:T(1024)S(1)} %add_divide_fusion, ...), kind=kOutput, calls=%fused_computation.107 | convolution fusion | flops 539820032 | bytes 17568128 | tf_op jit(solution)/shard_map/transpose(jvp())/dot_general | solution.py:57
  159.5 15.0 %all_gather.25 = bf16[256,1024]{1,0:T(8,128)(2,1)S(1)} all-gather(bf16[32,1024]{1,0:T(8,128)(2,1)S(1)} %add_convert_fusion.1), channel_id=1, replica_groups=mesh['ctx'=4,'frame'=8] {'frame'}, dimensions={0}, use_global_device_ids=true | all-gather | bytes 589824 | tf_op jit(solution)/shard_map/all_gather | solution.py:151
  175.5 11.6 %all_gather.26 = bf16[1024,256]{1,0:T(8,128)(2,1)} all-gather(bf16[256,256]{1,0:T(8,128)(2,1)S(1)} %bitcast.48), channel_id=1, replica_groups=mesh['ctx'=4,'frame'=8] {'ctx'}, dimensions={0}, use_global_device_ids=true | all-gather | bytes 655360 | tf_op jit(solution)/shard_map/all_gather | solution.py:170
  187.5 7.7 %all_gather.27 = f32[1024,2]{0,1:T(2,128)S(1)} all-gather(f32[256,2]{0,1:T(2,128)S(1)} %pad_maximum_fusion.9), channel_id=1, replica_groups=mesh['ctx'=4,'frame'=8] {'ctx'}, dimensions={0}, use_global_device_ids=true | all-gather | bytes 10240 | tf_op jit(solution)/shard_map/all_gather | solution.py:174
  195.2 3.8 %multiply_convert_fusion.1 = bf16[1024,1024]{1,0:T(8,128)(2,1)S(1)} fusion(f32[1024,1024]{1,0:T(8,128)} %fusion.67, f32[1024]{0:T(1024)S(1)} %bitcast.65, f32[1024]{0:T(1024)S(1)} %bitcast.62, pred[1024]{0:T(1024)(128)(4,1)S(1)} %dynamic_slice.6, bf16[1024,256]{1,0:T(8,128)(2,1)} %param.14, bf16[1024,256]{1,0:T(8,128)(2,1)} %all_gather.26), kind=kOutput, calls=%fused_computation.10 | convolution fusion | flops 275775488 | bytes 6824960 | tf_op jit(solution)/shard_map/dot_general | solution.py:184
  199.9 1.8 multiply_convert_fusion
  205.0 3.4 %fusion.11 = f32[1024,128]{0,1:T(8,128)S(1)} fusion(f32[1024,1024]{1,0:T(8,128)} %fusion.67, f32[1024]{0:T(1024)S(1)} %bitcast.63, pred[1024]{0:T(1024)(128)(4,1)S(1)} %dynamic_slice.6, bf16[1024,256]{1,0:T(8,128)(2,1)} %all_gather.26), kind=kOutput, calls=%fused_computation.23 | convolution fusion | flops 272629760 | bytes 4985856 | tf_op jit(solution)/shard_map/dot_general | solution.py:50
  208.5 2.1 fusion.9
  211.6 2.5 %copy.40 = f32[1024,256]{1,0:T(8,128)} copy(f32[1024,256]{0,1:T(8,128)} %pad_maximum_fusion.3) | data formatting | bytes 2097152
  214.6 2.1 fusion.60
  219.8 10.4 %reduce-scatter.5.cloned.1.call-done = f32[256,256]{0,1:T(8,128)} async-done(((f32[1024,256]{0,1:T(8,128)}), f32[256,256]{0,1:T(8,128)}) %reduce-scatter.5.cloned.1.call-update) | async-done | bytes 262160 | tf_op jit(solution)/shard_map/reduce_scatter | solution.py:204
  (124 shorter events, 31.2 us)
Async XLA Ops:
  7.2 86.5 %copy-start = (bf16[256,1024]{1,0:T(8,128)(2,1)S(1)}, bf16[256,1024]{1,0:T(8,128)(2,1)}, u32[]{:S(2)}) copy-start(bf16[256,1024]{1,0:T(8,128)(2,1)} %param.18) | copy-start | bytes 1572868
  7.2 5.0 %copy-start.19 = (s32[16]{0:T(128)S(1)}, s32[16]{0:T(128)}, u32[]{:S(2)}) copy-start(s32[16]{0:T(128)} %param.15) | copy-start | bytes 196
  7.2 5.2 %copy-start.15 = (bf16[256,256]{1,0:T(8,128)(2,1)S(1)}, bf16[256,256]{1,0:T(8,128)(2,1)}, u32[]{:S(2)}) copy-start(bf16[256,256]{1,0:T(8,128)(2,1)} %param.12) | copy-start | bytes 393220
  7.2 5.3 %copy-start.17 = (s32[256]{0:T(256)S(1)}, s32[256]{0:T(256)}, u32[]{:S(2)}) copy-start(s32[256]{0:T(256)} %param.16) | copy-start | bytes 3076
  7.2 5.5 %copy-start.18 = (s32[16]{0:T(128)S(1)}, s32[16]{0:T(128)}, u32[]{:S(2)}) copy-start(s32[16]{0:T(128)} %param.17) | copy-start | bytes 196
  7.2 42.4 %all-gather.3.cloned.1.call-start = ((), (), s32[]{:S(2)}) async-start(), calls=%async_computation.2 | async-start | bytes 2621440 | tf_op jit(solution)/shard_map/all_gather | solution.py:97
  11.4 75.4 %all-gather.5.cloned.1.call-start = ((), (), s32[]{:S(2)}) async-start(), calls=%async_computation.3 | async-start | bytes 2621440 | tf_op jit(solution)/shard_map/all_gather | solution.py:98
  12.2 115.3 %reduce-scatter.3.cloned.1.call-start = ((), (), s32[]{:S(2)}) async-start(), calls=%async_computation.4 | async-start | bytes 1179648 | tf_op jit(solution)/shard_map/reduce_scatter | solution.py:138
  49.6 3.0 %copy-start.11 = (bf16[4096,256]{0,1:T(8,128)(2,1)S(1)}, bf16[4096,256]{0,1:T(8,128)(2,1)}, u32[]{:S(2)}) copy-start(bf16[4096,256]{0,1:T(8,128)(2,1)} %all-gather.3.cloned.1.call-done) | copy-start | bytes 6291460
  51.9 1.9 copy-start.1
  53.8 2.0 copy-start.2
  86.8 3.8 %copy-start.3 = (f32[256,4096]{1,0:T(8,128)S(1)}, f32[256,4096]{1,0:T(8,128)}, u32[]{:S(2)}) copy-start(f32[256,4096]{1,0:T(8,128)} %copy-done.2) | copy-start | bytes 12582916
  90.6 19.2 %copy-start.5 = (bf16[1024,2,128]{0,2,1:T(8,128)(2,1)S(1)}, bf16[1024,2,128]{0,2,1:T(8,128)(2,1)}, u32[]{:S(2)}) copy-start(bf16[1024,2,128]{0,2,1:T(8,128)(2,1)} %pad_maximum_fusion.4) | copy-start | bytes 1572868
  94.9 135.2 %reduce-scatter.5.cloned.1.call-start = ((), (), s32[]{:S(2)}) async-start(), calls=%async_computation.5 | async-start | bytes 1310720 | tf_op jit(solution)/shard_map/reduce_scatter | solution.py:204
  109.0 6.1 %copy-start.6 = (bf16[1024,256]{0,1:T(8,128)(2,1)}, bf16[1024,256]{0,1:T(8,128)(2,1)S(1)}, u32[]{:S(2)}) copy-start(bf16[1024,256]{0,1:T(8,128)(2,1)S(1)} %all_gather.21) | copy-start | bytes 1572868
  134.6 8.9 %copy-start.16 = (f32[1024]{0:T(1024)S(1)}, f32[1024]{0:T(1024)}, u32[]{:S(2)}) copy-start(f32[1024]{0:T(1024)} %param.21) | copy-start | bytes 12292
  134.6 13.5 %copy-start.8 = (f32[32,1024]{1,0:T(8,128)S(1)}, f32[32,1024]{1,0:T(8,128)}, u32[]{:S(2)}) copy-start(f32[32,1024]{1,0:T(8,128)} %reduce-scatter.3.cloned.1.call-done) | copy-start | bytes 393220
  195.2 4.7 %copy-start.9 = (f32[1024,1024]{1,0:T(8,128)S(1)}, f32[1024,1024]{1,0:T(8,128)}, u32[]{:S(2)}) copy-start(f32[1024,1024]{1,0:T(8,128)} %fusion.58) | copy-start | bytes 12582916
  195.2 4.7 %copy-start.13 = (bf16[1024,256]{1,0:T(8,128)(2,1)S(1)}, bf16[1024,256]{1,0:T(8,128)(2,1)}, u32[]{:S(2)}) copy-start(bf16[1024,256]{1,0:T(8,128)(2,1)} %all_gather.26) | copy-start | bytes 1572868
  195.2 4.7 %copy-start.14 = (bf16[1024,256]{1,0:T(8,128)(2,1)S(1)}, bf16[1024,256]{1,0:T(8,128)(2,1)}, u32[]{:S(2)}) copy-start(bf16[1024,256]{1,0:T(8,128)(2,1)} %param.14) | copy-start | bytes 1572868
  201.7 1.4 copy-start.4
  205.0 3.5 %copy-start.10 = (f32[1024,1024]{1,0:T(8,128)S(1)}, f32[1024,1024]{1,0:T(8,128)}, u32[]{:S(2)}) copy-start(f32[1024,1024]{1,0:T(8,128)} %fusion.58) | copy-start | bytes 12582916
  208.5 5.7 %copy-start.7 = (bf16[1024,256]{0,1:T(8,128)(2,1)S(1)}, bf16[1024,256]{0,1:T(8,128)(2,1)}, u32[]{:S(2)}) copy-start(bf16[1024,256]{0,1:T(8,128)(2,1)} %copy-done.6) | copy-start | bytes 1572868
  214.2 2.6 %copy-start.12 = (f32[1024,64]{0,1:T(8,128)S(1)}, f32[1024,64]{0,1:T(8,128)}, u32[]{:S(2)}) copy-start(f32[1024,64]{0,1:T(8,128)} %get-tuple-element.37) | copy-start | bytes 786436
Sparse Core Ops, SparseCore 0:
  11.5 38.0 all-gather.2
  51.5 35.2 all-gather.4
  95.1 32.3 reduce-scatter.2
  205.1 25.0 reduce-scatter.4
where the time goes:
time: 240 us
  waiting for transfers between devices  82.7 us (34%)
  blocking collectives  55 us (23%)
  matrix products  52.2 us (22%)
  between operations  19.5 us (8%)
  other arithmetic  18.3 us (8%)
  local copies, waits for them, and re-layouts  11.9 us (5%)
    all_gather x1, waiting for transfers between devices, shards(): lax.all_gather(rotated_key, 'ctx', axis=0, tiled=True)  36.2 us
    all_gather x1, waiting for transfers between devices, shards(): lax.all_gather(values, 'ctx', axis=0, tiled=True)  30.3 us
    dot_general x2, matrix products, score_clip(): jnp.dot(normed, mlp_up, preferred_element_type=jnp.float32)  16.1 us
    all_gather x1, blocking collectives, shards(): lax.all_gather(low_grad, 'frame', axis=0, tiled=True)  15 us
    all_gather x1, blocking collectives, shards(): lax.all_gather(rotated_query, 'ctx', axis=0, tiled=True)  13.4 us
    all_gather x1, blocking collectives, shards(): lax.all_gather(out_grad, 'ctx', axis=0, tiled=True)  11.6 us
    reduce_scatter x1, waiting for transfers between devices, shards(): lax.psum_scatter(jnp.concatenate(query_parts, axis=1), 'ctx', scatter_dim...  10.4 us
    dot_general x4, matrix products, head_scores(): jnp.dot(query_head, key_head.T, preferred_element_type=jnp.float32)  8.48 us
  transfers between devices with their start and end apart: 4, of which 4 were waited for; matrix products, arithmetic and copies ran while one was open for 11% of the time, Pallas kernels for 0%

commit v1 on v0

v1 whole, which is shorter than its diff:
```python
import functools
import math

import jax
import jax.numpy as jnp
import numpy as np
from jax import lax
from jax.experimental import pallas as pl
from jax.experimental.pallas import tpu as pltpu
from jax.sharding import PartitionSpec as P

HD = 128
FTOK = 16
CLIP = 2
EPSILON = 1e-05
NEG = -1e30
LOG2E = math.log2(math.e)
MESH = pl.DeviceIdType.MESH
BF = jnp.bfloat16
F32 = jnp.float32
VCHUNK = 512

NN = (((1,), (0,)), ((), ()))
NT = (((1,), (1,)), ((), ()))


def mm(left, right, dims):
    return lax.dot_general(left, right, dims, preferred_element_type=F32)


def iota(shape, dim):
    return lax.broadcasted_iota(jnp.int32, shape, dim)


def norm_stats(x):
    center = jnp.mean(x, axis=-1, keepdims=True)
    centered = x - center
    inverse = lax.rsqrt(jnp.mean(centered * centered, axis=-1, keepdims=True) + EPSILON)
    return centered * inverse, inverse


def norm_back(grad, hat, inverse):
    return inverse * (
        grad
        - jnp.mean(grad, axis=-1, keepdims=True)
        - hat * jnp.mean(grad * hat, axis=-1, keepdims=True)
    )


def kernel(
    n_ctx,
    n_frame,
    q_ref,
    k_ref,
    v_ref,
    qf_ref,
    fc_ref,
    cf_ref,
    ck_ref,
    sk_ref,
    cq_ref,
    sq_ref,
    ct_ref,
    st_ref,
    ip_ref,
    up_ref,
    down_ref,
    head_ref,
    dq_ref,
    dk_ref,
    dv_ref,
    rew_ref,
    kin,
    vin,
    ip,
    up,
    down,
    qbuf,
    kr,
    krt,
    vt,
    cosk,
    sink,
    osend,
    orecv,
    ssend,
    srecv,
    ot,
    xsend,
    xrecv,
    gbuf,
    gp,
    dobuf,
    sbuf,
    dqsend,
    dqrecv,
    csend,
    crecv,
    fsend,
    frecv,
    local,
):
    me = lax.axis_index("ctx")
    fi = lax.axis_index("frame")
    rows, width = q_ref.shape
    key_rows = k_ref.shape[0]
    heads = width // HD
    slots = qf_ref.shape[1]
    clip_rows = CLIP * FTOK
    vd = ip_ref.shape[1]
    vff = up_ref.shape[1]
    scale = 1.0 / math.sqrt(HD)

    loads = [
        pltpu.make_async_copy(src, dst, local.at[i])
        for i, (src, dst) in enumerate(
            [(k_ref, kin), (v_ref, vin), (ip_ref, ip), (up_ref, up), (down_ref, down)]
        )
    ]
    for load in loads:
        load.start()

    barrier = pltpu.get_barrier_semaphore()
    for d in range(1, n_ctx):
        pl.semaphore_signal(
            barrier, inc=1, device_id={"ctx": lax.rem(me + d, n_ctx)}, device_id_type=MESH
        )
    for d in range(1, n_frame):
        pl.semaphore_signal(
            barrier, inc=1, device_id={"frame": lax.rem(fi + d, n_frame)}, device_id_type=MESH
        )

    def send_ctx(phase, src, dst, offset, index):
        return pltpu.make_async_remote_copy(
            src_ref=src,
            dst_ref=dst,
            send_sem=csend.at[phase, index],
            recv_sem=crecv.at[phase, offset],
            device_id={"ctx": lax.rem(me + offset, n_ctx)},
            device_id_type=MESH,
        )

    def send_frame(phase, src, dst, d):
        return pltpu.make_async_remote_copy(
            src_ref=src,
            dst_ref=dst,
            send_sem=fsend.at[phase, d],
            recv_sem=frecv.at[phase, d],
            device_id={"frame": lax.rem(fi + d, n_frame)},
            device_id_type=MESH,
        )

    def table(cos_a, sin_a, cos_b, sin_b):
        n_a = cos_a.shape[0]
        cos_a, sin_a = cos_a[:, None, :], sin_a[:, None, :]
        cos_b, sin_b = cos_b[None], sin_b[None]
        return (
            (cos_a * cos_b - sin_a * sin_b).reshape(n_a * FTOK, HD),
            (sin_a * cos_b + cos_a * sin_b).reshape(n_a * FTOK, HD),
        )

    cos_t, sin_t = ct_ref[...], st_ref[...]
    cos_q, sin_q = table(cq_ref[...], sq_ref[...], cos_t, sin_t)
    for h in range(heads):
        part = q_ref[:, h * HD : (h + 1) * HD].astype(F32)
        qbuf[0, :, h * HD : (h + 1) * HD] = (
            part * cos_q + pltpu.roll(part, HD // 2, 1) * sin_q
        ).astype(BF)

    pl.semaphore_wait(barrier, n_ctx - 1 + n_frame - 1)
    q_sends = [send_ctx(0, qbuf.at[0], qbuf.at[d], d, d) for d in range(1, n_ctx)]
    for copy in q_sends:
        copy.start()

    cos_k, sin_k = table(ck_ref[...], sk_ref[...], cos_t, sin_t)
    cosk[...] = cos_k
    sink[...] = sin_k
    loads[0].wait()
    loads[1].wait()
    for h in range(heads):
        part = kin[:, h * HD : (h + 1) * HD].astype(F32)
        turned = (part * cosk[...] + pltpu.roll(part, HD // 2, 1) * sink[...]).astype(BF)
        kr[:, h * HD : (h + 1) * HD] = turned
        krt[h * HD : (h + 1) * HD, :] = turned.astype(F32).T.astype(BF)
        vt[h * HD : (h + 1) * HD, :] = vin[:, h * HD : (h + 1) * HD].astype(F32).T.astype(BF)

    live_total = jnp.sum(fc_ref[...].astype(F32), axis=1, keepdims=True)
    key_at = (iota((key_rows, 1), 0) + me * key_rows).astype(F32)
    bias = jnp.where(key_at < live_total, 0.0, NEG)

    def forward(d, out_ref, stat_ref):
        for h in range(heads):
            cols = slice(h * HD, (h + 1) * HD)
            s = mm(kr[:, cols], qbuf[d, :, cols], NT) * (scale * LOG2E) + bias
            top = jnp.max(s, axis=0, keepdims=True)
            p = jnp.exp2(s - top)
            total = jnp.sum(p, axis=0, keepdims=True)
            o = mm(vt[cols, :], p.astype(BF), NN) * (1.0 / total)
            out_ref[cols, :] = o.astype(BF)
            stat_ref[h : h + 1, :] = top + jnp.log2(total)

    ssend[...] = jnp.zeros_like(ssend)
    forward(0, orecv.at[0], srecv.at[0])

    def o_copies(d):
        back = n_ctx - d
        return (
            send_ctx(1, osend.at[d], orecv.at[back], back, d),
            send_ctx(2, ssend.at[d], srecv.at[back], back, d),
        )

    @pl.loop(1, n_ctx)
    def _(d):
        send_ctx(0, qbuf.at[0], qbuf.at[d], d, d).wait_recv()
        forward(d, osend.at[d], ssend.at[d])
        for copy in o_copies(d):
            copy.start()

    clip_row = cf_ref[...].astype(F32)
    eye = iota((slots, slots), 0) == iota((slots, slots), 1)
    clip_col = jnp.sum(jnp.where(eye, clip_row, 0.0), axis=1, keepdims=True)
    frame_col = jnp.sum(jnp.where(eye, qf_ref[...].astype(F32), 0.0), axis=1, keepdims=True)
    earlier = jnp.logical_and(
        clip_col == clip_row, iota((slots, slots), 1) < iota((slots, slots), 0)
    )
    dest_col = clip_col * CLIP + jnp.sum(jnp.where(earlier, 1.0, 0.0), axis=1, keepdims=True)
    dest_row = jnp.sum(jnp.where(eye, dest_col, 0.0), axis=0, keepdims=True)
    wide_row = (
        jnp.sum(
            jnp.where(iota((slots, rows), 0) == lax.div(iota((slots, rows), 1), FTOK), dest_col, 0.0),
            axis=0,
            keepdims=True,
        )
        * FTOK
        + lax.rem(iota((1, rows), 1), FTOK).astype(F32)
    )
    wide_col = (
        jnp.sum(
            jnp.where(lax.div(iota((rows, slots), 0), FTOK) == iota((rows, slots), 1), dest_row, 0.0),
            axis=1,
            keepdims=True,
        )
        * FTOK
        + lax.rem(iota((rows, 1), 0), FTOK).astype(F32)
    )
    to_group = jnp.where(iota((rows, rows), 0).astype(F32) == wide_row, 1.0, 0.0).astype(BF)
    from_group = jnp.where(iota((rows, rows), 1).astype(F32) == wide_col, 1.0, 0.0).astype(BF)
    count_col = jnp.clip(live_total - frame_col * FTOK, 0.0, float(FTOK))
    live = jnp.zeros((clip_rows, 1), F32)
    count = jnp.zeros((1, 1), F32)
    for j in range(CLIP):
        mine = (fi * CLIP + j).astype(F32)
        tokens = jnp.sum(jnp.where(dest_col == mine, count_col, 0.0), axis=0, keepdims=True)
        at = (iota((clip_rows, 1), 0) - j * FTOK).astype(F32)
        live = live + jnp.where(jnp.logical_and(at >= 0.0, at < tokens), 1.0, 0.0)
        count = count + tokens

    loads[2].wait()
    for d in range(1, n_ctx):
        send_ctx(1, osend.at[d], orecv.at[d], d, d).wait_recv()
        send_ctx(2, ssend.at[d], srecv.at[d], d, d).wait_recv()
    sbuf[0] = jnp.zeros_like(sbuf[0])
    for h in range(heads):
        cols = slice(h * HD, (h + 1) * HD)
        logs = [srecv[c, h : h + 1, :] for c in range(n_ctx)]
        top = functools.reduce(jnp.maximum, logs)
        shares = [jnp.exp2(x - top) for x in logs]
        total = functools.reduce(jnp.add, shares)
        inverse = 1.0 / total
        acc = jnp.zeros((HD, rows), F32)
        for c in range(n_ctx):
            acc = acc + orecv[c, cols, :].astype(F32) * (shares[c] * inverse)
        ot[cols, :] = acc.astype(BF)
        sbuf[0, h : h + 1, :] = top + jnp.log2(total)

    grouped = mm(to_group, ot[...], NT).astype(BF)
    shares = mm(grouped, ip[...], NN).astype(BF)
    for f in range(n_frame):
        xsend[f] = shares[f * clip_rows : (f + 1) * clip_rows, :]
    x_sends = [
        send_frame(0, xsend.at[lax.rem(fi + d, n_frame)], xrecv.at[d], d) for d in range(1, n_frame)
    ]
    for copy in x_sends:
        copy.start()
    x = xsend[fi].astype(F32)
    for d in range(1, n_frame):
        x_sends[d - 1].wait_recv()
        x = x + xrecv[d].astype(F32)

    hat, inverse = norm_stats(x)
    y = hat.astype(BF)
    loads[3].wait()
    loads[4].wait()
    c0 = math.sqrt(2.0 / math.pi)
    c1 = 0.044715

    def mlp_step(j, hidden):
        cols = pl.ds(pl.multiple_of(j * VCHUNK, VCHUNK), VCHUNK)
        u = mm(y, up[:, cols], NN)
        t = jnp.tanh(c0 * (u + c1 * u * u * u))
        e = (0.5 * u * (1.0 + t)).astype(BF)
        gp[:, cols] = 0.5 * (1.0 + t) + 0.5 * u * (1.0 - t * t) * (c0 * (1.0 + 3.0 * c1 * u * u))
        return hidden + mm(e, down[cols, :], NN)

    hidden = lax.fori_loop(0, vff // VCHUNK, mlp_step, jnp.zeros((clip_rows, vd), F32))
    pooled = jnp.sum(hidden * live, axis=0, keepdims=True) / count
    pooled_hat, pooled_inverse = norm_stats(pooled)
    weight = head_ref[...]
    rew_ref[...] = count * jnp.sum(pooled_hat * weight, axis=1, keepdims=True)
    d_hidden = norm_back(weight, pooled_hat, pooled_inverse)
    high = d_hidden.astype(BF).astype(F32)
    pick = iota((16, vd), 0)
    pair = jnp.where(
        pick == 0, high, jnp.where(pick == 1, d_hidden - high, 0.0)
    ).astype(BF)

    def back_step(j, d_y):
        cols = pl.ds(pl.multiple_of(j * VCHUNK, VCHUNK), VCHUNK)
        both = mm(pair, down[cols, :], NT)
        d_e = both[0:1, :] + both[1:2, :]
        d_u = (live * d_e * gp[:, cols]).astype(BF)
        return d_y + mm(d_u, up[:, cols], NT)

    d_y = lax.fori_loop(0, vff // VCHUNK, back_step, jnp.zeros((clip_rows, vd), F32))
    gbuf[fi] = norm_back(d_y, hat, inverse).astype(BF)
    g_sends = [send_frame(1, gbuf.at[fi], gbuf.at[fi], d) for d in range(1, n_frame)]
    for copy in g_sends:
        copy.start()
    for d in range(1, n_frame):
        source = lax.rem(fi + n_frame - d, n_frame)
        send_frame(1, gbuf.at[source], gbuf.at[source], d).wait_recv()
    g = gbuf[...].reshape(rows, vd)
    grouped_grad = mm(g, ip[...], NT).astype(BF)
    out_grad = mm(from_group, grouped_grad, NN)
    dobuf[0] = out_grad.astype(BF)
    for h in range(heads):
        cols = slice(h * HD, (h + 1) * HD)
        turned = out_grad[:, cols].T
        sbuf[0, heads + h : heads + h + 1, :] = jnp.sum(
            turned * ot[cols, :].astype(F32), axis=0, keepdims=True
        )
    do_sends = []
    for d in range(1, n_ctx):
        do_sends.append(send_ctx(3, dobuf.at[0], dobuf.at[d], d, d))
        do_sends.append(send_ctx(4, sbuf.at[0], sbuf.at[d], d, d))
    for copy in do_sends:
        copy.start()

    def backward(d, out_ref, first):
        for h in range(heads):
            cols = slice(h * HD, (h + 1) * HD)
            q_head = qbuf[d, :, cols]
            do_head = dobuf[d, :, cols]
            s = mm(kr[:, cols], q_head, NT) * (scale * LOG2E) + bias
            p = jnp.exp2(s - sbuf[d, h : h + 1, :])
            dp = mm(vin[:, cols], do_head, NT)
            ds = (p * (dp - sbuf[d, heads + h : heads + h + 1, :]) * scale).astype(BF)
            dv = mm(p.astype(BF), do_head, NN)
            dk = mm(ds, q_head, NN)
            if first:
                dv_ref[:, cols] = dv
                dk_ref[:, cols] = dk
            else:
                dv_ref[:, cols] = dv_ref[:, cols] + dv
                dk_ref[:, cols] = dk_ref[:, cols] + dk
            out_ref[cols, :] = mm(krt[cols, :], ds, NN).astype(BF)

    backward(0, dqrecv.at[0], True)

    def dq_copy(d):
        back = n_ctx - d
        return send_ctx(5, dqsend.at[d], dqrecv.at[back], back, d)

    @pl.loop(1, n_ctx)
    def _(d):
        send_ctx(3, dobuf.at[0], dobuf.at[d], d, d).wait_recv()
        send_ctx(4, sbuf.at[0], sbuf.at[d], d, d).wait_recv()
        backward(d, dqsend.at[d], False)
        dq_copy(d).start()

    for h in range(heads):
        cols = slice(h * HD, (h + 1) * HD)
        part = dk_ref[:, cols]
        dk_ref[:, cols] = part * cosk[...] - pltpu.roll(part, HD // 2, 1) * sink[...]

    for d in range(1, n_ctx):
        send_ctx(5, dqsend.at[d], dqrecv.at[d], d, d).wait_recv()
    cos_q, sin_q = table(cq_ref[...], sq_ref[...], ct_ref[...], st_ref[...])
    for h in range(heads):
        cols = slice(h * HD, (h + 1) * HD)
        acc = dqrecv[0, cols, :].astype(F32)
        for c in range(1, n_ctx):
            acc = acc + dqrecv[c, cols, :].astype(F32)
        part = acc.T
        dq_ref[:, cols] = part * cos_q - pltpu.roll(part, HD // 2, 1) * sin_q

    for copy in q_sends + x_sends + g_sends + do_sends:
        copy.wait_send()
    for d in range(1, n_ctx):
        for copy in o_copies(d):
            copy.wait_send()
        dq_copy(d).wait_send()


def shards(
    n_ctx,
    n_frame,
    queries,
    keys,
    values,
    query_frames,
    frame_counts,
    clip_of_frame,
    in_proj,
    mlp_up,
    mlp_down,
    reward_head,
):
    rows, width = queries.shape
    key_rows = keys.shape[0]
    key_frames = key_rows // FTOK
    vd, vff = mlp_up.shape
    half = HD // 2
    clip_rows = CLIP * FTOK
    lane = np.arange(HD) % half
    frequency = jnp.asarray(
        np.exp(-math.log(10000.0) * lane / half).astype(np.float32)
    )
    sign = jnp.asarray(np.where(np.arange(HD) < half, -1.0, 1.0).astype(np.float32))

    def trig(position):
        angle = position.astype(F32)[:, None] * frequency[None, :]
        return jnp.cos(angle), jnp.sin(angle) * sign[None, :]

    first_frame = lax.axis_index("ctx") * key_frames
    cos_k, sin_k = trig((first_frame + jnp.arange(key_frames, dtype=jnp.int32)) * FTOK)
    cos_q, sin_q = trig(query_frames * FTOK)
    cos_t, sin_t = trig(jnp.arange(FTOK, dtype=jnp.int32))

    vmem = pl.BlockSpec(memory_space=pltpu.VMEM)
    hbm = pl.BlockSpec(memory_space=pl.ANY)
    call = pl.pallas_call(
        functools.partial(kernel, n_ctx, n_frame),
        out_shape=(
            jax.ShapeDtypeStruct((rows, width), F32),
            jax.ShapeDtypeStruct((key_rows, width), F32),
            jax.ShapeDtypeStruct((key_rows, width), F32),
            jax.ShapeDtypeStruct((1, 1), F32),
        ),
        in_specs=[vmem, hbm, hbm] + [vmem] * 9 + [hbm] * 3 + [vmem],
        out_specs=(vmem, vmem, vmem, vmem),
        scratch_shapes=[
            pltpu.VMEM((key_rows, width), BF),
            pltpu.VMEM((key_rows, width), BF),
            pltpu.VMEM((width, vd), BF),
            pltpu.VMEM((vd, vff), BF),
            pltpu.VMEM((vff, vd), BF),
            pltpu.VMEM((n_ctx, rows, width), BF),
            pltpu.VMEM((key_rows, width), BF),
            pltpu.VMEM((width, key_rows), BF),
            pltpu.VMEM((width, key_rows), BF),
            pltpu.VMEM((key_rows, HD), F32),
            pltpu.VMEM((key_rows, HD), F32),
            pltpu.VMEM((n_ctx, width, rows), BF),
            pltpu.VMEM((n_ctx, width, rows), BF),
            pltpu.VMEM((n_ctx, 8, rows), F32),
            pltpu.VMEM((n_ctx, 8, rows), F32),
            pltpu.VMEM((width, rows), BF),
            pltpu.VMEM((n_frame, clip_rows, vd), BF),
            pltpu.VMEM((n_frame, clip_rows, vd), BF),
            pltpu.VMEM((n_frame, clip_rows, vd), BF),
            pltpu.VMEM((clip_rows, vff), F32),
            pltpu.VMEM((n_ctx, rows, width), BF),
            pltpu.VMEM((n_ctx, 8, rows), F32),
            pltpu.VMEM((n_ctx, width, rows), BF),
            pltpu.VMEM((n_ctx, width, rows), BF),
            pltpu.SemaphoreType.DMA((6, n_ctx)),
            pltpu.SemaphoreType.DMA((6, n_ctx)),
            pltpu.SemaphoreType.DMA((2, n_frame)),
            pltpu.SemaphoreType.DMA((2, n_frame)),
            pltpu.SemaphoreType.DMA((5,)),
        ],
        compiler_params=pltpu.CompilerParams(
            collective_id=0, has_side_effects=True, vmem_limit_bytes=60 * 1024 * 1024
        ),
    )
    query_grad, key_grad, value_grad, reward = call(
        queries,
        keys,
        values,
        query_frames.reshape(1, -1),
        frame_counts.reshape(1, -1),
        clip_of_frame.reshape(1, -1),
        cos_k,
        sin_k,
        cos_q,
        sin_q,
        cos_t,
        sin_t,
        in_proj,
        mlp_up,
        mlp_down,
        reward_head.reshape(1, -1),
    )
    return query_grad, key_grad, value_grad, reward.reshape(1)


def solution(mesh):
    return jax.shard_map(
        functools.partial(shards, mesh.shape["ctx"], mesh.shape["frame"]),
        mesh=mesh,
        in_specs=(
            P("ctx", "frame"),
            P("ctx", "frame"),
            P("ctx", "frame"),
            P("ctx"),
            P(),
            P("ctx"),
            P("frame", None),
            P(),
            P(),
            P(),
        ),
        out_specs=(P("ctx", "frame"), P("ctx", "frame"), P("ctx", "frame"), P(("ctx", "frame"))),
        check_vma=False,
    )
```

time: 240 us -> 86.3 us (0.36)
  waiting for transfers between devices: 82.7 us -> 0 us
  Pallas kernels: 0 us -> 73 us
  blocking collectives: 55 us -> 0 us
  matrix products: 52.2 us -> 0 us
  between operations: 19.5 us -> 2.4 us
  other arithmetic: 18.3 us -> 3.58 us
  local copies, waits for them, and re-layouts: 11.9 us -> 6.19 us
    pallas_call x0 -> x1, Pallas kernels: none -> 73 us  [shards(): call(queries, keys, values, query_frames.reshape(1, -1), frame_counts.res...]
    all_gather x2 -> x0, waiting for transfers between devices: 66.5 us -> none  [the longest x1 36.2 us: shards(): lax.all_gather(rotated_key, 'ctx', axis=0, tiled=True)]
    all_gather x5 -> x0, blocking collectives: 55 us -> none  [the longest x1 15 us: shards(): lax.all_gather(low_grad, 'frame', axis=0, tiled=True)]
    dot_general x19 -> x0, matrix products: 52.2 us -> none  [the longest x2 16.1 us: score_clip(): jnp.dot(normed, mlp_up, preferred_element_type=jnp.float32)]
    reduce_scatter x2 -> x0, waiting for transfers between devices: 15.4 us -> none  [the longest x1 10.4 us: shards(): lax.psum_scatter(jnp.concatenate(query_parts, axis=1), 'ctx', scatter_dim...]
    reduce_sum x15 -> x0, other arithmetic: 9.02 us -> none  [the longest x2 2.35 us: normalize(): variance = jnp.mean(centered * centered, axis=-1, keepdims=True)]
    reshape x4 -> x0, local copies, waits for them, and re-layouts: 3.55 us -> none  [the longest x2 2.15 us: rotate(): return result.reshape(row_count, -1)]
    concatenate x8 -> x0, other arithmetic: 3.17 us -> none  [the longest x1 1.05 us: shards(): jnp.concatenate(query_parts, axis=1)]
  transfers between devices with their start and end apart: 4 -> 0, of which waited for: 4 -> 0; matrix products, arithmetic and copies ran while one was open for 11% -> 0% of each run, Pallas kernels for 0% -> 0%
where the time goes in v1:
time: 86.3 us; the launch traced here: 85.2 us
  Pallas kernels  73 us (85%)
  local copies, waits for them, and re-layouts  6.19 us (7%)
  other arithmetic  3.58 us (4%)
  between operations  2.4 us (3%)
    pallas_call x1, Pallas kernels, shards(): call(queries, keys, values, query_frames.reshape(1, -1), frame_counts.res...  73 us
    unnamed x3, local copies, waits for them, and re-layouts  6.19 us
    mul x2, other arithmetic, trig(): return (jnp.cos(angle), jnp.sin(angle) * sign[None, :])  2.92 us

profile of v1, /device:TPU:0, one launch (start us, length us, event | category | flops | bytes accessed | tf_op | source)
XLA Modules:
  0.0 85.2 jit_solution(9639736843666376260)
XLA Ops:
  0.6 0.7 iota_convert_fusion
  1.3 1.4 %fusion.2 = (f32[16,128]{1,0:T(8,128)}, f32[16,128]{1,0:T(8,128)}, f32[16,128]{1,0:T(8,128)}, f32[16,128]{1,0:T(8,128)}) fusion(f32[16]{0:T(128)S(1)} %get-tuple-element.18, f32[128]{0:T(128)} %constant.15.clone, f32[128]{0:T(128)} %constant.14.clone, f32[16]{0:T(128)S(1)} %get-tuple-element.19), kind=kLoop, calls=%fused_computation.8 | loop fusion | flops 8192 | bytes 33920 | tf_op jit(solution)/shard_map/mul | solution.py:433
  2.7 1.5 %fusion = (f32[64,128]{1,0:T(8,128)}, f32[64,128]{1,0:T(8,128)}) fusion(f32[128]{0:T(128)} %constant.15.clone, f32[128]{0:T(128)} %constant.14.clone, f32[64]{0:T(128)S(1)} %multiply_convert_fusion.1), kind=kLoop, calls=%fused_computation.2 | loop fusion | flops 16384 | bytes 66816 | tf_op jit(solution)/shard_map/mul | solution.py:433
  4.2 73.0 %shard_map.147 = (f32[256,256]{1,0:T(8,128)}, f32[1024,256]{1,0:T(8,128)}, f32[1024,256]{1,0:T(8,128)}, f32[1,1]{1,0:T(1,128)}) custom-call(bf16[256,256]{1,0:T(8,128)(2,1)} %q_ref.1, bf16[1024,256]{1,0:T(8,128)(2,1)} %k_ref.1, bf16[1024,256]{1,0:T(8,128)(2,1)} %v_ref.1, s32[1,16]{1,0:T(1,128)} %bitcast.7, s32[1,256]{1,0:T(1,128)} %bitcast.6, ...), custom_call_target="tpu_custom_call" | custom-call | tf_op jit(solution)/shard_map/pallas_call | solution.py:487
  77.3 1.7 %copy.20 = f32[256,256]{1,0:T(8,128)} copy(f32[256,256]{1,0:T(8,128)} %get-tuple-element.24) | data formatting | bytes 524288
  78.9 2.3 %copy.21 = f32[1024,256]{1,0:T(8,128)} copy(f32[1024,256]{1,0:T(8,128)} %get-tuple-element.25) | data formatting | bytes 2097152
  81.2 2.3 %copy.22 = f32[1024,256]{1,0:T(8,128)} copy(f32[1024,256]{1,0:T(8,128)} %get-tuple-element.26) | data formatting | bytes 2097152
  (1 shorter events, 0.0 us)

commit v2 on v1

--- a/solution.py
+++ b/solution.py
@@ -19,6 +19,7 @@
 BF = jnp.bfloat16
 F32 = jnp.float32
 VCHUNK = 512
+PIECES = 4
 
 NN = (((1,), (0,)), ((), ()))
 NT = (((1,), (1,)), ((), ()))
@@ -56,12 +57,8 @@
     qf_ref,
     fc_ref,
     cf_ref,
-    ck_ref,
-    sk_ref,
-    cq_ref,
-    sq_ref,
-    ct_ref,
-    st_ref,
+    cos_ref,
+    sin_ref,
     ip_ref,
     up_ref,
     down_ref,
@@ -76,23 +73,29 @@
     up,
     down,
     qbuf,
-    kr,
     krt,
     vt,
     cosk,
     sink,
+    cosq,
+    sinq,
     osend,
     orecv,
     ssend,
     srecv,
     ot,
     xsend,
+    xpair,
+    xsum,
     xrecv,
     gbuf,
     gp,
     dobuf,
+    lbuf,
     sbuf,
-    dqsend,
+    stash,
+    dkacc,
+    dvacc,
     dqrecv,
     csend,
     crecv,
@@ -109,7 +112,14 @@
     clip_rows = CLIP * FTOK
     vd = ip_ref.shape[1]
     vff = up_ref.shape[1]
+    key_frames = key_rows // FTOK
     scale = 1.0 / math.sqrt(HD)
+    n_deep = n_frame // 2
+    core, deep = lax.rem(fi, 2), lax.div(fi, 2)
+    sibling = fi + 1 - 2 * core
+
+    def deep_peer(d):
+        return lax.rem(deep + d, n_deep) * 2 + core
 
     loads = [
         pltpu.make_async_copy(src, dst, local.at[i])
@@ -125,10 +135,8 @@
         pl.semaphore_signal(
             barrier, inc=1, device_id={"ctx": lax.rem(me + d, n_ctx)}, device_id_type=MESH
         )
-    for d in range(1, n_frame):
-        pl.semaphore_signal(
-            barrier, inc=1, device_id={"frame": lax.rem(fi + d, n_frame)}, device_id_type=MESH
-        )
+    for peer in [sibling] + [deep_peer(d) for d in range(1, n_deep)]:
+        pl.semaphore_signal(barrier, inc=1, device_id={"frame": peer}, device_id_type=MESH)
 
     def send_ctx(phase, src, dst, offset, index):
         return pltpu.make_async_remote_copy(
@@ -140,13 +148,13 @@
             device_id_type=MESH,
         )
 
-    def send_frame(phase, src, dst, d):
+    def send_frame(phase, src, dst, peer, d):
         return pltpu.make_async_remote_copy(
             src_ref=src,
             dst_ref=dst,
             send_sem=fsend.at[phase, d],
             recv_sem=frecv.at[phase, d],
-            device_id={"frame": lax.rem(fi + d, n_frame)},
+            device_id={"frame": peer},
             device_id_type=MESH,
         )
 
@@ -159,20 +167,37 @@
             (sin_a * cos_b + cos_a * sin_b).reshape(n_a * FTOK, HD),
         )
 
-    cos_t, sin_t = ct_ref[...], st_ref[...]
-    cos_q, sin_q = table(cq_ref[...], sq_ref[...], cos_t, sin_t)
+    all_frames = cos_ref.shape[0] - FTOK
+    cos_t, sin_t = cos_ref[all_frames:, :], sin_ref[all_frames:, :]
+    eye = iota((slots, slots), 0) == iota((slots, slots), 1)
+    frame_col = jnp.sum(jnp.where(eye, qf_ref[...].astype(F32), 0.0), axis=1, keepdims=True)
+    choose = jnp.where(iota((slots, all_frames), 1).astype(F32) == frame_col, 1.0, 0.0)
+
+    def chosen(ref):
+        return lax.dot_general(
+            choose,
+            ref[:all_frames, :],
+            NN,
+            precision=lax.Precision.HIGHEST,
+            preferred_element_type=F32,
+        )
+
+    cos_q, sin_q = table(chosen(cos_ref), chosen(sin_ref), cos_t, sin_t)
+    cosq[...] = cos_q
+    sinq[...] = sin_q
     for h in range(heads):
         part = q_ref[:, h * HD : (h + 1) * HD].astype(F32)
         qbuf[0, :, h * HD : (h + 1) * HD] = (
             part * cos_q + pltpu.roll(part, HD // 2, 1) * sin_q
         ).astype(BF)
 
-    pl.semaphore_wait(barrier, n_ctx - 1 + n_frame - 1)
+    pl.semaphore_wait(barrier, n_ctx - 1 + n_deep)
     q_sends = [send_ctx(0, qbuf.at[0], qbuf.at[d], d, d) for d in range(1, n_ctx)]
     for copy in q_sends:
         copy.start()
 
-    cos_k, sin_k = table(ck_ref[...], sk_ref[...], cos_t, sin_t)
+    own_frames = pl.ds(pl.multiple_of(me * key_frames, 8), key_frames)
+    cos_k, sin_k = table(cos_ref[own_frames, :], sin_ref[own_frames, :], cos_t, sin_t)
     cosk[...] = cos_k
     sink[...] = sin_k
     loads[0].wait()
@@ -180,7 +205,7 @@
     for h in range(heads):
         part = kin[:, h * HD : (h + 1) * HD].astype(F32)
         turned = (part * cosk[...] + pltpu.roll(part, HD // 2, 1) * sink[...]).astype(BF)
-        kr[:, h * HD : (h + 1) * HD] = turned
+        kin[:, h * HD : (h + 1) * HD] = turned
         krt[h * HD : (h + 1) * HD, :] = turned.astype(F32).T.astype(BF)
         vt[h * HD : (h + 1) * HD, :] = vin[:, h * HD : (h + 1) * HD].astype(F32).T.astype(BF)
 
@@ -191,7 +216,7 @@
     def forward(d, out_ref, stat_ref):
         for h in range(heads):
             cols = slice(h * HD, (h + 1) * HD)
-            s = mm(kr[:, cols], qbuf[d, :, cols], NT) * (scale * LOG2E) + bias
+            s = mm(kin[:, cols], qbuf[d, :, cols], NT) * (scale * LOG2E) + bias
             top = jnp.max(s, axis=0, keepdims=True)
             p = jnp.exp2(s - top)
             total = jnp.sum(p, axis=0, keepdims=True)
@@ -217,9 +242,7 @@
             copy.start()
 
     clip_row = cf_ref[...].astype(F32)
-    eye = iota((slots, slots), 0) == iota((slots, slots), 1)
     clip_col = jnp.sum(jnp.where(eye, clip_row, 0.0), axis=1, keepdims=True)
-    frame_col = jnp.sum(jnp.where(eye, qf_ref[...].astype(F32), 0.0), axis=1, keepdims=True)
     earlier = jnp.logical_and(
         clip_col == clip_row, iota((slots, slots), 1) < iota((slots, slots), 0)
     )
@@ -259,6 +282,7 @@
     for d in range(1, n_ctx):
         send_ctx(1, osend.at[d], orecv.at[d], d, d).wait_recv()
         send_ctx(2, ssend.at[d], srecv.at[d], d, d).wait_recv()
+    lbuf[0] = jnp.zeros_like(lbuf[0])
     sbuf[0] = jnp.zeros_like(sbuf[0])
     for h in range(heads):
         cols = slice(h * HD, (h + 1) * HD)
@@ -271,19 +295,41 @@
         for c in range(n_ctx):
             acc = acc + orecv[c, cols, :].astype(F32) * (shares[c] * inverse)
         ot[cols, :] = acc.astype(BF)
-        sbuf[0, h : h + 1, :] = top + jnp.log2(total)
+        lbuf[0, h : h + 1, :] = top + jnp.log2(total)
+    l_sends = [send_ctx(6, lbuf.at[0], lbuf.at[d], d, d) for d in range(1, n_ctx)]
+    for copy in l_sends:
+        copy.start()
 
     grouped = mm(to_group, ot[...], NT).astype(BF)
     shares = mm(grouped, ip[...], NN).astype(BF)
     for f in range(n_frame):
-        xsend[f] = shares[f * clip_rows : (f + 1) * clip_rows, :]
+        xsend[f % 2, f // 2] = shares[f * clip_rows : (f + 1) * clip_rows, :]
+    pair_send = send_frame(3, xsend.at[1 - core], xpair, sibling, 0)
+    pair_send.start()
+    pair_send.wait_recv()
+    xsum[...] = (xsend[core].astype(F32) + xpair[...].astype(F32)).astype(BF)
     x_sends = [
-        send_frame(0, xsend.at[lax.rem(fi + d, n_frame)], xrecv.at[d], d) for d in range(1, n_frame)
+        send_frame(0, xsum.at[lax.rem(deep + d, n_deep)], xrecv.at[d], deep_peer(d), d)
+        for d in range(1, n_deep)
     ]
     for copy in x_sends:
         copy.start()
-    x = xsend[fi].astype(F32)
-    for d in range(1, n_frame):
+
+    def keep_weights(d):
+        for h in range(heads):
+            cols = slice(h * HD, (h + 1) * HD)
+            s = mm(kin[:, cols], qbuf[d, :, cols], NT) * (scale * LOG2E) + bias
+            stash[d * heads + h] = jnp.exp2(s - lbuf[d, h : h + 1, :]).astype(BF)
+
+    keep_weights(0)
+
+    @pl.loop(1, n_ctx)
+    def _(d):
+        send_ctx(6, lbuf.at[0], lbuf.at[d], d, d).wait_recv()
+        keep_weights(d)
+
+    x = xsend[core, deep].astype(F32) + xpair[deep].astype(F32)
+    for d in range(1, n_deep):
         x_sends[d - 1].wait_recv()
         x = x + xrecv[d].astype(F32)
 
@@ -323,12 +369,19 @@
 
     d_y = lax.fori_loop(0, vff // VCHUNK, back_step, jnp.zeros((clip_rows, vd), F32))
     gbuf[fi] = norm_back(d_y, hat, inverse).astype(BF)
-    g_sends = [send_frame(1, gbuf.at[fi], gbuf.at[fi], d) for d in range(1, n_frame)]
+    g_sends = [send_frame(1, gbuf.at[fi], gbuf.at[fi], deep_peer(d), d) for d in range(1, n_deep)]
+    g_sends.append(send_frame(2, gbuf.at[fi], gbuf.at[fi], sibling, 0))
     for copy in g_sends:
         copy.start()
-    for d in range(1, n_frame):
-        source = lax.rem(fi + n_frame - d, n_frame)
-        send_frame(1, gbuf.at[source], gbuf.at[source], d).wait_recv()
+    for d in range(1, n_deep):
+        source = deep_peer(n_deep - d)
+        send_frame(1, gbuf.at[source], gbuf.at[source], deep_peer(d), d).wait_recv()
+        forward_copy = send_frame(2, gbuf.at[source], gbuf.at[source], sibling, d)
+        forward_copy.start()
+        g_sends.append(forward_copy)
+    for d in range(n_deep):
+        source = lax.rem(deep + n_deep - d, n_deep) * 2 + 1 - core
+        send_frame(2, gbuf.at[source], gbuf.at[source], sibling, d).wait_recv()
     g = gbuf[...].reshape(rows, vd)
     grouped_grad = mm(g, ip[...], NT).astype(BF)
     out_grad = mm(from_group, grouped_grad, NN)
@@ -336,7 +389,7 @@
     for h in range(heads):
         cols = slice(h * HD, (h + 1) * HD)
         turned = out_grad[:, cols].T
-        sbuf[0, heads + h : heads + h + 1, :] = jnp.sum(
+        sbuf[0, h : h + 1, :] = jnp.sum(
             turned * ot[cols, :].astype(F32), axis=0, keepdims=True
         )
     do_sends = []
@@ -351,55 +404,91 @@
             cols = slice(h * HD, (h + 1) * HD)
             q_head = qbuf[d, :, cols]
             do_head = dobuf[d, :, cols]
-            s = mm(kr[:, cols], q_head, NT) * (scale * LOG2E) + bias
-            p = jnp.exp2(s - sbuf[d, h : h + 1, :])
+            p = stash[d * heads + h]
             dp = mm(vin[:, cols], do_head, NT)
-            ds = (p * (dp - sbuf[d, heads + h : heads + h + 1, :]) * scale).astype(BF)
-            dv = mm(p.astype(BF), do_head, NN)
+            ds = (p.astype(F32) * (dp - sbuf[d, h : h + 1, :]) * scale).astype(BF)
+            dv = mm(p, do_head, NN)
             dk = mm(ds, q_head, NN)
             if first:
-                dv_ref[:, cols] = dv
-                dk_ref[:, cols] = dk
+                dvacc[:, cols] = dv
+                dkacc[:, cols] = dk
             else:
-                dv_ref[:, cols] = dv_ref[:, cols] + dv
-                dk_ref[:, cols] = dk_ref[:, cols] + dk
+                dvacc[:, cols] = dvacc[:, cols] + dv
+                dkacc[:, cols] = dkacc[:, cols] + dk
             out_ref[cols, :] = mm(krt[cols, :], ds, NN).astype(BF)
 
+    for d in range(1, n_ctx):
+        for copy in o_copies(d):
+            copy.wait_send()
     backward(0, dqrecv.at[0], True)
 
     def dq_copy(d):
         back = n_ctx - d
-        return send_ctx(5, dqsend.at[d], dqrecv.at[back], back, d)
+        return send_ctx(5, osend.at[d], dqrecv.at[back], back, d)
 
     @pl.loop(1, n_ctx)
     def _(d):
         send_ctx(3, dobuf.at[0], dobuf.at[d], d, d).wait_recv()
         send_ctx(4, sbuf.at[0], sbuf.at[d], d, d).wait_recv()
-        backward(d, dqsend.at[d], False)
+        backward(d, osend.at[d], False)
         dq_copy(d).start()
 
+    dv_store = pltpu.make_async_copy(dvacc, dv_ref, local.at[5])
+    dv_store.start()
     for h in range(heads):
         cols = slice(h * HD, (h + 1) * HD)
-        part = dk_ref[:, cols]
-        dk_ref[:, cols] = part * cosk[...] - pltpu.roll(part, HD // 2, 1) * sink[...]
-
+        part = dkacc[:, cols]
+        dkacc[:, cols] = part * cosk[...] - pltpu.roll(part, HD // 2, 1) * sink[...]
+
+    dk_store = pltpu.make_async_copy(dkacc, dk_ref, local.at[6])
+    dk_store.start()
     for d in range(1, n_ctx):
-        send_ctx(5, dqsend.at[d], dqrecv.at[d], d, d).wait_recv()
-    cos_q, sin_q = table(cq_ref[...], sq_ref[...], ct_ref[...], st_ref[...])
+        send_ctx(5, osend.at[d], dqrecv.at[d], d, d).wait_recv()
     for h in range(heads):
         cols = slice(h * HD, (h + 1) * HD)
         acc = dqrecv[0, cols, :].astype(F32)
         for c in range(1, n_ctx):
             acc = acc + dqrecv[c, cols, :].astype(F32)
         part = acc.T
-        dq_ref[:, cols] = part * cos_q - pltpu.roll(part, HD // 2, 1) * sin_q
-
-    for copy in q_sends + x_sends + g_sends + do_sends:
+        dq_ref[:, cols] = part * cosq[...] - pltpu.roll(part, HD // 2, 1) * sinq[...]
+
+    for copy in q_sends + l_sends + [pair_send] + x_sends + g_sends + do_sends:
         copy.wait_send()
+    dv_store.wait()
+    dk_store.wait()
     for d in range(1, n_ctx):
-        for copy in o_copies(d):
-            copy.wait_send()
         dq_copy(d).wait_send()
+
+
+def deliver_kernel(*refs):
+    count = (len(refs) - 1) // 2
+    sems = refs[-1]
+    copies = []
+    for i in range(count):
+        for j in range(PIECES):
+            step = refs[i].shape[0] // PIECES
+            part = pl.ds(j * step, step)
+            copies.append(
+                pltpu.make_async_copy(
+                    refs[i].at[part], refs[count + i].at[part], sems.at[i * PIECES + j]
+                )
+            )
+    for copy in copies:
+        copy.start()
+    for copy in copies:
+        copy.wait()
+
+
+def deliver(*arrays):
+    hbm = pl.BlockSpec(memory_space=pl.ANY)
+    return pl.pallas_call(
+        deliver_kernel,
+        out_shape=tuple(jax.ShapeDtypeStruct(a.shape, a.dtype) for a in arrays),
+        in_specs=[hbm] * len(arrays),
+        out_specs=(hbm,) * len(arrays),
+        scratch_shapes=[pltpu.SemaphoreType.DMA((len(arrays) * PIECES,))],
+        compiler_params=pltpu.CompilerParams(vmem_limit_bytes=60 * 1024 * 1024),
+    )(*arrays)
 
 
 def shards(
@@ -418,24 +507,19 @@
 ):
     rows, width = queries.shape
     key_rows = keys.shape[0]
-    key_frames = key_rows // FTOK
     vd, vff = mlp_up.shape
     half = HD // 2
+    heads = width // HD
+    n_deep = n_frame // 2
     clip_rows = CLIP * FTOK
     lane = np.arange(HD) % half
-    frequency = jnp.asarray(
-        np.exp(-math.log(10000.0) * lane / half).astype(np.float32)
-    )
-    sign = jnp.asarray(np.where(np.arange(HD) < half, -1.0, 1.0).astype(np.float32))
-
-    def trig(position):
-        angle = position.astype(F32)[:, None] * frequency[None, :]
-        return jnp.cos(angle), jnp.sin(angle) * sign[None, :]
-
-    first_frame = lax.axis_index("ctx") * key_frames
-    cos_k, sin_k = trig((first_frame + jnp.arange(key_frames, dtype=jnp.int32)) * FTOK)
-    cos_q, sin_q = trig(query_frames * FTOK)
-    cos_t, sin_t = trig(jnp.arange(FTOK, dtype=jnp.int32))
+    frequency = np.exp(-math.log(10000.0) * lane / half).astype(np.float32)
+    sign = np.where(np.arange(HD) < half, -1.0, 1.0)
+
+    position = np.concatenate([np.arange(frame_counts.shape[0]) * FTOK, np.arange(FTOK)])
+    angle = (position.astype(np.float32)[:, None] * frequency[None, :]).astype(np.float64)
+    cosines = jnp.asarray(np.cos(angle).astype(np.float32))
+    sines = jnp.asarray((np.sin(angle) * sign[None, :]).astype(np.float32))
 
     vmem = pl.BlockSpec(memory_space=pltpu.VMEM)
     hbm = pl.BlockSpec(memory_space=pl.ANY)
@@ -447,8 +531,8 @@
             jax.ShapeDtypeStruct((key_rows, width), F32),
             jax.ShapeDtypeStruct((1, 1), F32),
         ),
-        in_specs=[vmem, hbm, hbm] + [vmem] * 9 + [hbm] * 3 + [vmem],
-        out_specs=(vmem, vmem, vmem, vmem),
+        in_specs=[vmem, hbm, hbm] + [vmem] * 5 + [hbm] * 3 + [vmem],
+        out_specs=(vmem, hbm, hbm, vmem),
         scratch_shapes=[
             pltpu.VMEM((key_rows, width), BF),
             pltpu.VMEM((key_rows, width), BF),
@@ -456,29 +540,35 @@
             pltpu.VMEM((vd, vff), BF),
             pltpu.VMEM((vff, vd), BF),
             pltpu.VMEM((n_ctx, rows, width), BF),
-            pltpu.VMEM((key_rows, width), BF),
             pltpu.VMEM((width, key_rows), BF),
             pltpu.VMEM((width, key_rows), BF),
             pltpu.VMEM((key_rows, HD), F32),
             pltpu.VMEM((key_rows, HD), F32),
+            pltpu.VMEM((rows, HD), F32),
+            pltpu.VMEM((rows, HD), F32),
             pltpu.VMEM((n_ctx, width, rows), BF),
             pltpu.VMEM((n_ctx, width, rows), BF),
             pltpu.VMEM((n_ctx, 8, rows), F32),
             pltpu.VMEM((n_ctx, 8, rows), F32),
             pltpu.VMEM((width, rows), BF),
-            pltpu.VMEM((n_frame, clip_rows, vd), BF),
-            pltpu.VMEM((n_frame, clip_rows, vd), BF),
+            pltpu.VMEM((2, n_deep, clip_rows, vd), BF),
+            pltpu.VMEM((n_deep, clip_rows, vd), BF),
+            pltpu.VMEM((n_deep, clip_rows, vd), BF),
+            pltpu.VMEM((n_deep, clip_rows, vd), BF),
             pltpu.VMEM((n_frame, clip_rows, vd), BF),
             pltpu.VMEM((clip_rows, vff), F32),
             pltpu.VMEM((n_ctx, rows, width), BF),
             pltpu.VMEM((n_ctx, 8, rows), F32),
+            pltpu.VMEM((n_ctx, 8, rows), F32),
+            pltpu.VMEM((n_ctx * heads, key_rows, rows), BF),
+            pltpu.VMEM((key_rows, width), F32),
+            pltpu.VMEM((key_rows, width), F32),
             pltpu.VMEM((n_ctx, width, rows), BF),
-            pltpu.VMEM((n_ctx, width, rows), BF),
-            pltpu.SemaphoreType.DMA((6, n_ctx)),
-            pltpu.SemaphoreType.DMA((6, n_ctx)),
-            pltpu.SemaphoreType.DMA((2, n_frame)),
-            pltpu.SemaphoreType.DMA((2, n_frame)),
-            pltpu.SemaphoreType.DMA((5,)),
+            pltpu.SemaphoreType.DMA((7, n_ctx)),
+            pltpu.SemaphoreType.DMA((7, n_ctx)),
+            pltpu.SemaphoreType.DMA((4, n_deep)),
+            pltpu.SemaphoreType.DMA((4, n_deep)),
+            pltpu.SemaphoreType.DMA((7,)),
         ],
         compiler_params=pltpu.CompilerParams(
             collective_id=0, has_side_effects=True, vmem_limit_bytes=60 * 1024 * 1024
@@ -491,17 +581,14 @@
         query_frames.reshape(1, -1),
         frame_counts.reshape(1, -1),
         clip_of_frame.reshape(1, -1),
-        cos_k,
-        sin_k,
-        cos_q,
-        sin_q,
-        cos_t,
-        sin_t,
+        cosines,
+        sines,
         in_proj,
         mlp_up,
         mlp_down,
         reward_head.reshape(1, -1),
     )
+    query_grad, key_grad, value_grad = deliver(query_grad, key_grad, value_grad)
     return query_grad, key_grad, value_grad, reward.reshape(1)
 
 

time: 86.3 us -> 142 us (1.65)
  Pallas kernels: 73 us -> 140 us
  local copies, waits for them, and re-layouts: 6.19 us -> 0 us
  other arithmetic: 3.58 us -> 0 us
    pallas_call x0 -> x1, Pallas kernels: none -> 72.7 us  [deliver(): pl.pallas_call(deliver_kernel, out_shape=tuple((jax.ShapeDtypeStruct(a.sh...]
    pallas_call x1, Pallas kernels: 73 us -> 66.8 us  [shards(): call(queries, keys, values, query_frames.reshape(1, -1), frame_counts.res...]
    unnamed x3 -> x0, local copies, waits for them, and re-layouts: 6.19 us -> none
    mul x2 -> x0, other arithmetic: 2.92 us -> none  [trig(): return (jnp.cos(angle), jnp.sin(angle) * sign[None, :])]
where the time goes in v2:
time: 142 us
  Pallas kernels  140 us (99%)
  between operations  2.46 us (2%)
    pallas_call x1, Pallas kernels, deliver(): pl.pallas_call(deliver_kernel, out_shape=tuple((jax.ShapeDtypeStruct(a.sh...  72.7 us
    pallas_call x1, Pallas kernels, shards(): call(queries, keys, values, query_frames.reshape(1, -1), frame_counts.res...  66.8 us

profile of v2, /device:TPU:0, one launch (start us, length us, event | category | flops | bytes accessed | tf_op | source)
XLA Modules:
  0.0 142.0 jit_solution(14153833589097105152)
XLA Ops:
  0.6 66.8 %shard_map.147 = (f32[256,256]{1,0:T(8,128)}, f32[1024,256]{1,0:T(8,128)}, f32[1024,256]{1,0:T(8,128)}, f32[1,1]{1,0:T(1,128)}) custom-call(bf16[256,256]{1,0:T(8,128)(2,1)} %q_ref.1, bf16[1024,256]{1,0:T(8,128)(2,1)} %k_ref.1, bf16[1024,256]{1,0:T(8,128)(2,1)} %v_ref.1, s32[1,16]{1,0:T(1,128)} %bitcast.7, s32[1,256]{1,0:T(1,128)} %bitcast.6, ...), custom_call_target="tpu_custom_call" | custom-call | tf_op jit(solution)/shard_map/pallas_call | solution.py:577
  67.5 72.7 %shard_map.148 = (f32[256,256]{1,0:T(8,128)}, f32[1024,256]{1,0:T(8,128)}, f32[1024,256]{1,0:T(8,128)}) custom-call(f32[256,256]{1,0:T(8,128)} %get-tuple-element.11.refs_0_, f32[1024,256]{1,0:T(8,128)} %get-tuple-element.12.refs_1_, f32[1024,256]{1,0:T(8,128)} %get-tuple-element.13.refs_2_), custom_call_target="tpu_custom_call" | custom-call | tf_op jit(solution)/shard_map/pallas_call | solution.py:484

commit v3 on v2

--- a/solution.py
+++ b/solution.py
@@ -461,32 +461,39 @@
 
 
 def deliver_kernel(*refs):
-    count = (len(refs) - 1) // 2
-    sems = refs[-1]
-    copies = []
+    count = (len(refs) - 2) // 3
+    held, sem_in, sem_out = refs[2 * count : 3 * count], refs[-2], refs[-1]
+    inward, outward = [], []
     for i in range(count):
+        step = refs[i].shape[0] // PIECES
         for j in range(PIECES):
-            step = refs[i].shape[0] // PIECES
             part = pl.ds(j * step, step)
-            copies.append(
-                pltpu.make_async_copy(
-                    refs[i].at[part], refs[count + i].at[part], sems.at[i * PIECES + j]
-                )
+            n = i * PIECES + j
+            inward.append(
+                pltpu.make_async_copy(refs[i].at[part], held[i].at[part], sem_in.at[n])
             )
-    for copy in copies:
+            outward.append(
+                pltpu.make_async_copy(held[i].at[part], refs[count + i].at[part], sem_out.at[n])
+            )
+    for copy in inward:
         copy.start()
-    for copy in copies:
+    for arrive, leave in zip(inward, outward):
+        arrive.wait()
+        leave.start()
+    for copy in outward:
         copy.wait()
 
 
 def deliver(*arrays):
     hbm = pl.BlockSpec(memory_space=pl.ANY)
+    copies = len(arrays) * PIECES
     return pl.pallas_call(
         deliver_kernel,
         out_shape=tuple(jax.ShapeDtypeStruct(a.shape, a.dtype) for a in arrays),
         in_specs=[hbm] * len(arrays),
         out_specs=(hbm,) * len(arrays),
-        scratch_shapes=[pltpu.SemaphoreType.DMA((len(arrays) * PIECES,))],
+        scratch_shapes=[pltpu.VMEM(a.shape, a.dtype) for a in arrays]
+        + [pltpu.SemaphoreType.DMA((copies,)), pltpu.SemaphoreType.DMA((copies,))],
         compiler_params=pltpu.CompilerParams(vmem_limit_bytes=60 * 1024 * 1024),
     )(*arrays)
 

time: 142 us -> 72.1 us (0.51)
  Pallas kernels: 140 us -> 69.4 us
    pallas_call x1, Pallas kernels: 72.7 us -> 2.61 us  [deliver(): pl.pallas_call(deliver_kernel, out_shape=tuple((jax.ShapeDtypeStruct(a.sh...]
where the time goes in v3:
time: 72.1 us; the launch traced here: 71.9 us
  Pallas kernels  69.4 us (96%)
  between operations  2.46 us (3%)
    pallas_call x1, Pallas kernels, shards(): call(queries, keys, values, query_frames.reshape(1, -1), frame_counts.res...  66.8 us
    pallas_call x1, Pallas kernels, deliver(): pl.pallas_call(deliver_kernel, out_shape=tuple((jax.ShapeDtypeStruct(a.sh...  2.61 us

profile of v3, /device:TPU:0, one launch (start us, length us, event | category | flops | bytes accessed | tf_op | source)
XLA Modules:
  0.0 71.9 jit_solution(15073392975439563112)
XLA Ops:
  0.6 66.8 %shard_map.147 = (f32[256,256]{1,0:T(8,128)}, f32[1024,256]{1,0:T(8,128)}, f32[1024,256]{1,0:T(8,128)}, f32[1,1]{1,0:T(1,128)}) custom-call(bf16[256,256]{1,0:T(8,128)(2,1)} %q_ref.1, bf16[1024,256]{1,0:T(8,128)(2,1)} %k_ref.1, bf16[1024,256]{1,0:T(8,128)(2,1)} %v_ref.1, s32[1,16]{1,0:T(1,128)} %bitcast.7, s32[1,256]{1,0:T(1,128)} %bitcast.6, ...), custom_call_target="tpu_custom_call" | custom-call | tf_op jit(solution)/shard_map/pallas_call | solution.py:584
  67.5 2.6 %shard_map.148 = (f32[256,256]{1,0:T(8,128)}, f32[1024,256]{1,0:T(8,128)}, f32[1024,256]{1,0:T(8,128)}) custom-call(f32[256,256]{1,0:T(8,128)} %get-tuple-element.11.refs_0_, f32[1024,256]{1,0:T(8,128)} %get-tuple-element.12.refs_1_, f32[1024,256]{1,0:T(8,128)} %get-tuple-element.13.refs_2_), custom_call_target="tpu_custom_call" | custom-call | tf_op jit(solution)/shard_map/pallas_call | solution.py:490
